TPU v7x, 32 devices: a whole 2x2x4 slice. The times are simulated.
32 devices in a mesh: tm: 4 (over y, x), agent: 8 (over z, core).
Axes of the slice: x: 2, y: 2, z: 4, core: 2. Of those that a mesh axis runs over, the one named last changes fastest.
Arguments:
- tokens: bfloat16 [16, 512, 1024], P('tm', 'agent'), may hold values from -6 to 6
- conv_taps: float32 [5, 1024], replicated, may hold values from -3 to 3
- norm_first: float32 [1024], replicated, may hold values from 0.1 to 1.9
- norm_second: float32 [1024], replicated, may hold values from 0.1 to 1.9
- norm_third: float32 [1024], replicated, may hold values from 0.1 to 1.9
- w_in: bfloat16 [1024, 3072], replicated, may hold values from -0.1875 to 0.1875
- w_out: bfloat16 [3072, 1024], replicated, may hold values from -0.109375 to 0.109375
- w_query: bfloat16 [1024, 1024], replicated, may hold values from -16 to 16
- w_key: bfloat16 [1024, 1024], replicated, may hold values from -16 to 16
- w_value: bfloat16 [1024, 1024], replicated, may hold values from -0.1875 to 0.1875
- w_output: bfloat16 [1024, 1024], replicated, may hold values from -0.1875 to 0.1875
- agent_order: int32 [512], P('agent'), may hold values from 0 to 511, each once
- present_steps: int32 [512], P('agent'), may hold values from 1 to 16
Outputs:
- result: bfloat16 [16, 512, 1024], P('tm', 'agent')
Inputs may be any that keep to these rules, and one draw needn't show every extreme that they name: `agent_order`: each of 0 to 511 appears once.
All inputs are finite; a program needn't handle non-finite values.
Results may differ from a plain program's by a relative error of at most 0.012.
Values may be sent and summed in bfloat16 or wider, within the bound.
No kernel may reach another device: no remote copies, remote signals or barrier semaphores. Data moves between devices by JAX's collectives and lax.ppermute only.
A program may use at most 192 MiB of HBM per device.

v0:
```python
import jax
import jax.numpy as jnp
from jax import lax
from jax.sharding import PartitionSpec as P

HEADS = 16


EPS = 1e-05


def shifted(shard, axis, by):
    count = lax.axis_size(axis)
    pairs = [(i, i + by) for i in range(count) if 0 <= i + by < count]
    return lax.ppermute(shard, axis, pairs)


def normed_rows(rows, gain):
    values = rows.astype(jnp.float32)
    scale = lax.rsqrt(jnp.mean(values * values, axis=-1, keepdims=True) + EPS)
    return values * scale * gain


def make_absorb(query, own_order, steps, heads_here, project):
    step_count, agent_count, width = query.shape
    head_size = width // heads_here
    scale = head_size ** (-0.5)
    split_query = query.reshape(step_count, agent_count, heads_here, head_size)
    init = (
        jnp.full((step_count, heads_here, agent_count), -1e30, jnp.float32),
        jnp.zeros((step_count, heads_here, agent_count), jnp.float32),
        jnp.zeros((step_count, agent_count, heads_here, head_size), jnp.float32),
    )

    def absorb(carry, piece, start):
        best, total, summed = carry
        key_piece, value_piece, order_piece, present_piece = project(piece)
        count = key_piece.shape[1]
        key_piece = key_piece.reshape(step_count, count, heads_here, head_size)
        value_piece = value_piece.reshape(step_count, count, heads_here, head_size)
        scores = (
            jnp.einsum(
                "sahd,sbhd->shab", split_query, key_piece, preferred_element_type=jnp.float32
            )
            * scale
        )
        other_order = order_piece[0]
        earlier = other_order[None, None, :] < own_order[None, :, None]
        alive = steps[:, None, None] < present_piece[0][None, None, :]
        itself = other_order[None, None, :] == own_order[None, :, None]
        visible = (earlier & alive | itself)[:, None]
        masked = jnp.where(visible, scores, -1e30)
        fresh = jnp.maximum(best, jnp.max(masked, axis=-1))
        weights = jnp.where(visible, jnp.exp(masked - fresh[..., None]), 0.0).astype(jnp.bfloat16)
        total = jnp.sum(weights.astype(jnp.float32), axis=-1)
        part_sum = jnp.einsum(
            "shab,sbhd->sahd", weights, value_piece, preferred_element_type=jnp.float32
        )
        summed = part_sum
        return (fresh, total, summed)

    return (absorb, init)


def finish(carry, shape):
    best, total, summed = carry
    attended = summed / jnp.transpose(total, (0, 2, 1))[..., None]
    return attended.astype(jnp.bfloat16).reshape(shape)


def identity_piece(piece):
    return piece


def per_device(
    tokens,
    conv_taps,
    norm_first,
    norm_second,
    norm_third,
    w_in,
    w_out,
    w_query,
    w_key,
    w_value,
    w_output,
    agent_order,
    present_steps,
):
    step_count, agent_count, width = tokens.shape
    reach = conv_taps.shape[0] - 1
    earlier_steps = shifted(tokens, "tm", 1)
    extended = normed_rows(jnp.concatenate([earlier_steps, tokens], axis=0), norm_first)
    mixed = jnp.zeros((step_count, agent_count, width), jnp.float32)
    for lag in range(reach + 1):
        mixed = mixed + conv_taps[lag] * extended[reach - lag : reach - lag + step_count]
    first = (tokens.astype(jnp.float32) + mixed).astype(jnp.bfloat16)
    flat = first.reshape(step_count * agent_count, width)
    inner = normed_rows(flat, norm_second).astype(jnp.bfloat16)
    hidden = jax.nn.gelu(
        jnp.dot(inner, w_in, preferred_element_type=jnp.float32), approximate=False
    ).astype(jnp.bfloat16)
    second = (
        flat.astype(jnp.float32) + jnp.dot(hidden, w_out, preferred_element_type=jnp.float32)
    ).astype(jnp.bfloat16)
    attn_in = normed_rows(second, norm_third).astype(jnp.bfloat16)
    query = (
        jnp.dot(attn_in, w_query, preferred_element_type=jnp.float32)
        .astype(jnp.bfloat16)
        .reshape(step_count, agent_count, width)
    )
    order_rows = agent_order.reshape(1, agent_count)
    present_rows = present_steps.reshape(1, agent_count)
    keys = (
        jnp.dot(attn_in, w_key, preferred_element_type=jnp.float32)
        .astype(jnp.bfloat16)
        .reshape(step_count, agent_count, width)
    )
    values = (
        jnp.dot(attn_in, w_value, preferred_element_type=jnp.float32)
        .astype(jnp.bfloat16)
        .reshape(step_count, agent_count, width)
    )
    keys, values = (keys, values)
    query, keys, values = (
        lax.all_to_all(query, "tm", split_axis=2, concat_axis=0, tiled=True),
        lax.all_to_all(keys, "tm", split_axis=2, concat_axis=0, tiled=True),
        lax.all_to_all(values, "tm", split_axis=2, concat_axis=0, tiled=True),
    )
    steps = jnp.arange(query.shape[0], dtype=jnp.int32)
    heads_here = HEADS // lax.axis_size("tm")
    absorb, init = make_absorb(query, agent_order, steps, heads_here, identity_piece)
    carry = absorb(
        init,
        (
            lax.all_gather(keys, "agent", axis=1, tiled=True),
            lax.all_gather(values, "agent", axis=1, tiled=True),
            lax.all_gather(order_rows, "agent", axis=1, tiled=True),
            lax.all_gather(present_rows, "agent", axis=1, tiled=True),
        ),
        jnp.int32(0),
    )
    attended = finish(carry, query.shape)
    attended = lax.all_to_all(attended, "tm", split_axis=0, concat_axis=2, tiled=True)
    projected = jnp.dot(
        attended.reshape(step_count * agent_count, width),
        w_output,
        preferred_element_type=jnp.float32,
    )
    result = second.astype(jnp.float32) + projected
    return result.astype(jnp.bfloat16).reshape(step_count, agent_count, width)


def solution(mesh):
    in_specs = (
        P("tm", "agent", None),
        P(),
        P(),
        P(),
        P(),
        P(),
        P(),
        P(),
        P(),
        P(),
        P(),
        P("agent"),
        P("agent"),
    )
    out_specs = P("tm", "agent", None)
    return jax.shard_map(
        per_device, mesh=mesh, in_specs=in_specs, out_specs=out_specs, check_vma=False
    )
```

profile of v0, /device:TPU:0, one launch (start us, length us, event | category | flops | bytes accessed | tf_op | source)
XLA Modules:
  0.0 191.4 jit_solution(14312280234153887234)
XLA Ops:
  6.5 5.1 %collective-permute-start = (bf16[4,64,1024]{2,1,0:T(8,128)(2,1)}, bf16[4,64,1024]{2,1,0:T(8,128)(2,1)S(1)}, u32[]{:S(2)}, u32[]{:S(2)}) collective-permute-start(bf16[4,64,1024]{2,1,0:T(8,128)(2,1)} %param.13), channel_id=1, source_target_pairs={{0,8},{8,16},{16,24},{1,9},{9,17},{17,25},{2,10},{10,18},{18,26},{... | collective-permute-start | bytes 1572872 | tf_op jit(solution)/shard_map/ppermute | solution.py:15
  11.7 1.0 fusion.100
  12.6 10.5 %collective-permute-done = bf16[4,64,1024]{2,1,0:T(8,128)(2,1)S(1)} collective-permute-done((bf16[4,64,1024]{2,1,0:T(8,128)(2,1)}, bf16[4,64,1024]{2,1,0:T(8,128)(2,1)S(1)}, u32[]{:S(2)}, u32[]{:S(2)}) %collective-permute-start) | collective-permute-done | bytes 524320 | tf_op jit(solution)/shard_map/ppermute | solution.py:15
  23.1 1.3 fusion.11
  24.5 1.3 fusion.12
  25.8 0.6 multiply_reduce_fusion
  26.5 0.2 fusion.63
  26.7 15.0 %fusion.53 = (f32[256]{0:T(256)S(1)}, bf16[256,1024]{1,0:T(8,128)(2,1)}) fusion(bf16[3072,1024]{1,0:T(8,128)(2,1)} %param.19, bf16[256,1024]{1,0:T(8,128)(2,1)S(1)} %fusion.63, bf16[1024,3072]{1,0:T(8,128)(2,1)} %param.18, bf16[256,1024]{1,0:T(8,128)(2,1)S(1)} %bitcast.71), kind=kOutput, calls=%fused_computation.70 | convolution fusion | flops 3273916160 | bytes 14156800 | tf_op jit(solution)/shard_map/dot_general | solution.py:104
  41.8 1.8 convolution_convert_fusion
  43.6 0.7 copy.31
  44.3 0.8 reshape.197
  45.2 12.4 %all_to_all.66 = bf16[4,2,32768]{2,1,0:T(2,128)(2,1)S(1)} all-to-all(bf16[4,2,32768]{2,1,0:T(2,128)(2,1)S(1)} %reshape.197), channel_id=1, replica_groups=mesh['tm'=4,'agent'=8] {'tm'}, dimensions={0} | all-to-all | bytes 1048576 | tf_op jit(solution)/shard_map/all_to_all | solution.py:127
  57.5 0.7 reshape.198
  58.3 0.7 copy.32
  59.0 0.9 all_to_all.58
  60.0 2.4 %convolution_convert_fusion.2 = bf16[256,1024]{1,0:T(8,128)(2,1)S(1)} fusion(bf16[1024,1024]{1,0:T(8,128)(2,1)} %param.22, bf16[256,1024]{1,0:T(8,128)(2,1)S(1)} %copy-done.10, f32[1024]{0:T(1024)S(1)} %copy-done.7, f32[256]{0:T(256)S(1)} %add_rsqrt_fusion.2), kind=kOutput, calls=%fused_computation.68 | convolution fusion | flops 538181632 | bytes 3150848 | tf_op jit(solution)/shard_map/dot_general | solution.py:120
  62.4 0.7 copy.25
  63.1 0.8 reshape.195
  64.0 9.7 %all_to_all.67 = bf16[4,2,32768]{2,1,0:T(2,128)(2,1)S(1)} all-to-all(bf16[4,2,32768]{2,1,0:T(2,128)(2,1)S(1)} %reshape.195), channel_id=1, replica_groups=mesh['tm'=4,'agent'=8] {'tm'}, dimensions={0} | all-to-all | bytes 1048576 | tf_op jit(solution)/shard_map/all_to_all | solution.py:128
  73.7 0.7 reshape.196
  74.4 0.7 copy.26
  75.1 0.9 all_to_all.51
  76.1 0.7 dynamic-slice
  77.5 0.2 dynamic-update-slice
  77.7 0.2 dynamic-update-slice.1
  77.9 9.8 %all-reduce.2 = (s32[512]{0:T(512)S(1)}, s32[512]{0:T(512)S(1)}) all-reduce(s32[512]{0:T(512)S(1)} %dynamic-update-slice, s32[512]{0:T(512)S(1)} %dynamic-update-slice.1), channel_id=2, replica_groups=mesh['tm'=4,'agent'=8] {'agent'}, use_global_device_ids=true, to_apply=%add | all-reduce | flops 1024 | bytes 8192
  87.7 0.1 broadcast_compare_fusion.1
  87.8 2.4 %convolution_convert_fusion.1 = bf16[256,1024]{1,0:T(8,128)(2,1)S(1)} fusion(bf16[1024,1024]{1,0:T(8,128)(2,1)} %param.20, bf16[256,1024]{1,0:T(8,128)(2,1)S(1)} %copy-done.10, f32[1024]{0:T(1024)S(1)} %copy-done.7, f32[256]{0:T(256)S(1)} %add_rsqrt_fusion.2), kind=kOutput, calls=%fused_computation.67 | convolution fusion | flops 538181632 | bytes 3150848 | tf_op jit(solution)/shard_map/dot_general | solution.py:108
  90.2 0.7 copy.28
  90.9 1.5 reshape.199
  92.4 3.5 %all-to-all-start.1 = ((bf16[4,2,32768]{2,1,0:T(2,128)(2,1)}), bf16[4,2,32768]{2,1,0:T(2,128)(2,1)S(1)}, u32[]{:S(2)}, u32[]{:S(2)}) async-start(bf16[4,2,32768]{2,1,0:T(2,128)(2,1)} %reshape.199), calls=%async_computation.1 | async-start | bytes 1048576 | tf_op jit(solution)/shard_map/all_to_all | solution.py:126
  95.9 0.4 and_or_fusion
  96.3 6.3 %all-to-all-done.1 = bf16[4,2,32768]{2,1,0:T(2,128)(2,1)S(1)} async-done(((bf16[4,2,32768]{2,1,0:T(2,128)(2,1)}), bf16[4,2,32768]{2,1,0:T(2,128)(2,1)S(1)}, u32[]{:S(2)}, u32[]{:S(2)}) %all-to-all-start.1) | async-done | bytes 524320 | tf_op jit(solution)/shard_map/all_to_all | solution.py:126
  102.6 0.7 reshape.200
  103.3 0.5 copy.30
  103.9 0.4 reshape.174
  104.3 2.8 %all-gather.7.cloned.1.call-done = bf16[16,512,256]{2,0,1:T(8,128)(2,1)} async-done(((bf16[16,64,256]{2,0,1:T(8,128)(2,1)}), bf16[16,512,256]{2,0,1:T(8,128)(2,1)}) %all-gather.7.cloned.1.call-update) | async-done | bytes 4194320 | tf_op jit(solution)/shard_map/all_gather | solution.py:136
  107.1 7.5 %copy.33 = bf16[16,512,256]{1,2,0:T(8,128)(2,1)} copy(bf16[16,512,256]{2,0,1:T(8,128)(2,1)} %all-gather.7.cloned.1.call-done) | data formatting | bytes 8388608 | tf_op jit(solution)/shard_map/all_gather | solution.py:136
  114.7 4.2 %fusion = (f32[16,4,64]{2,1,0:T(4,128)S(1)}, f32[16,4,64,512]{3,2,1,0:T(8,128)S(1)}) fusion(pred[16,64,512]{2,1,0:T(8,128)(4,1)S(1)} %and_or_fusion, bf16[16,512,4,64]{1,3,2,0:T(8,128)(2,1)} %bitcast.63, bf16[16,64,4,64]{3,2,1,0:T(4,128)(2,1)S(1)} %reshape.174), kind=kOutput, calls=%fused_computation.3 | convolution fusion | flops 274722816 | bytes 13647872 | tf_op jit(solution)/shard_map/sahd,sbhd->shab/dot_general | solution.py:42
  118.9 3.2 %copy-done.2 = f32[16,4,64,512]{3,2,1,0:T(8,128)} copy-done((f32[16,4,64,512]{3,2,1,0:T(8,128)}, f32[16,4,64,512]{3,2,1,0:T(8,128)S(1)}, u32[]{:S(2)}) %copy-start.2) | copy-done | bytes 8388632
  122.1 2.8 %convert_reduce_fusion = f32[16,4,64]{2,1,0:T(4,128)S(1)} fusion(f32[16,4,64]{2,1,0:T(4,128)S(1)} %broadcast_maximum_fusion, f32[16,4,64,512]{3,2,1,0:T(8,128)S(1)} %get-tuple-element.19, pred[16,64,512]{2,1,0:T(8,128)(4,1)S(1)} %and_or_fusion), kind=kLoop, calls=%fused_computation | loop fusion | flops 14675968 | bytes 8945664 | tf_op jit(solution)/shard_map/reduce_sum | solution.py:55
  124.9 29.7 %all-gather.5.cloned.1.call-done = bf16[16,512,256]{2,0,1:T(8,128)(2,1)} async-done(((bf16[16,64,256]{2,0,1:T(8,128)(2,1)}), bf16[16,512,256]{2,0,1:T(8,128)(2,1)}) %all-gather.5.cloned.1.call-update) | async-done | bytes 4194320 | tf_op jit(solution)/shard_map/all_gather | solution.py:137
  154.7 7.6 %copy.27 = bf16[16,512,256]{1,2,0:T(8,128)(2,1)} copy(bf16[16,512,256]{2,0,1:T(8,128)(2,1)} %all-gather.5.cloned.1.call-done) | data formatting | bytes 8388608 | tf_op jit(solution)/shard_map/all_gather | solution.py:137
  162.2 7.3 %fusion.13 = bf16[16,64,4,64]{1,3,2,0:T(8,128)(2,1)S(1)} fusion(bf16[16,512,4,64]{1,3,2,0:T(8,128)(2,1)} %bitcast.70, f32[16,64,4]{1,2,0:T(4,128)S(1)} %bitcast.79, f32[16,4,64,512]{3,2,1,0:T(8,128)} %copy-done.2, f32[16,4,64]{2,1,0:T(4,128)S(1)} %broadcast_maximum_fusion, pred[16,64,512]{2,1,0:T(8,128)(4,1)S(1)} %and_or_fusion), kind=kOutput, calls=%fused_computation.28 | convolution fusion | flops 279445504 | bytes 13664256 | tf_op jit(solution)/shard_map/shab,sbhd->sahd/dot_general | solution.py:56
  169.5 0.3 copy.35
  169.9 12.6 %all_to_all.68 = bf16[16,64,256]{2,1,0:T(8,128)(2,1)S(1)} all-to-all(bf16[16,64,256]{2,1,0:T(8,128)(2,1)S(1)} %copy.35), channel_id=1, replica_groups=mesh['tm'=4,'agent'=8] {'tm'}, dimensions={0} | all-to-all | bytes 1048576 | tf_op jit(solution)/shard_map/all_to_all | solution.py:144
  182.5 0.4 copy.36
  183.1 1.5 fusion.49
  (34 shorter events, 0.4 us)
Async XLA Ops:
  6.5 35.3 %copy-start = (bf16[1024,1024]{1,0:T(8,128)(2,1)S(1)}, bf16[1024,1024]{1,0:T(8,128)(2,1)}, u32[]{:S(2)}) copy-start(bf16[1024,1024]{1,0:T(8,128)(2,1)} %param.21) | copy-start | bytes 6291460
  6.5 19.3 %copy-start.3 = (bf16[4,64,1024]{2,1,0:T(8,128)(2,1)S(1)}, bf16[4,64,1024]{2,1,0:T(8,128)(2,1)}, u32[]{:S(2)}) copy-start(bf16[4,64,1024]{2,1,0:T(8,128)(2,1)} %param.13) | copy-start | bytes 1572868
  6.5 100.6 %all-gather.7.cloned.1.call-start = ((), (), s32[]{:S(2)}) async-start(), calls=%async_computation.5 | async-start | bytes 4718592 | tf_op jit(solution)/shard_map/all_gather | solution.py:136
  6.5 16.6 %collective-permute-start = (bf16[4,64,1024]{2,1,0:T(8,128)(2,1)}, bf16[4,64,1024]{2,1,0:T(8,128)(2,1)S(1)}, u32[]{:S(2)}, u32[]{:S(2)}) collective-permute-start(bf16[4,64,1024]{2,1,0:T(8,128)(2,1)} %param.13), channel_id=1, source_target_pairs={{0,8},{8,16},{16,24},{1,9},{9,17},{17,25},{2,10},{10,18},{18,26},{... | collective-permute-start | bytes 1572872 | tf_op jit(solution)/shard_map/ppermute | solution.py:15
  25.8 0.7 copy-start.4
  26.7 15.1 %copy-start.7 = (f32[1024]{0:T(1024)S(1)}, f32[1024]{0:T(1024)}, u32[]{:S(2)}) copy-start(f32[1024]{0:T(1024)} %param.17) | copy-start | bytes 12292
  45.2 14.8 %copy-start.10 = (bf16[256,1024]{1,0:T(8,128)(2,1)S(1)}, bf16[256,1024]{1,0:T(8,128)(2,1)}, u32[]{:S(2)}) copy-start(bf16[256,1024]{1,0:T(8,128)(2,1)} %get-tuple-element.17) | copy-start | bytes 1572868
  60.0 94.7 %all-gather.5.cloned.1.call-start = ((), (), s32[]{:S(2)}) async-start(), calls=%async_computation.4 | async-start | bytes 4718592 | tf_op jit(solution)/shard_map/all_gather | solution.py:137
  64.0 12.1 %copy-start.9 = (u32[32]{0:T(128)S(1)}, u32[32]{0:T(128)}, u32[]{:S(2)}) copy-start(u32[32]{0:T(128)} %constant.79) | copy-start | bytes 388
  64.0 13.5 %copy-start.5 = (s32[64]{0:T(128)S(1)}, s32[64]{0:T(128)}, u32[]{:S(2)}) copy-start(s32[64]{0:T(128)} %param.24) | copy-start | bytes 772
  64.0 13.7 %copy-start.8 = (s32[64]{0:T(128)S(1)}, s32[64]{0:T(128)}, u32[]{:S(2)}) copy-start(s32[64]{0:T(128)} %param.25) | copy-start | bytes 772
  92.4 10.2 %all-to-all-start.1 = ((bf16[4,2,32768]{2,1,0:T(2,128)(2,1)}), bf16[4,2,32768]{2,1,0:T(2,128)(2,1)S(1)}, u32[]{:S(2)}, u32[]{:S(2)}) async-start(bf16[4,2,32768]{2,1,0:T(2,128)(2,1)} %reshape.199), calls=%async_computation.1 | async-start | bytes 1048576 | tf_op jit(solution)/shard_map/all_to_all | solution.py:126
  118.9 3.2 %copy-start.2 = (f32[16,4,64,512]{3,2,1,0:T(8,128)}, f32[16,4,64,512]{3,2,1,0:T(8,128)S(1)}, u32[]{:S(2)}) copy-start(f32[16,4,64,512]{3,2,1,0:T(8,128)S(1)} %get-tuple-element.19) | copy-start | bytes 25165828
  169.9 13.2 %copy-start.6 = (bf16[1024,1024]{1,0:T(8,128)(2,1)S(1)}, bf16[1024,1024]{1,0:T(8,128)(2,1)}, u32[]{:S(2)}) copy-start(bf16[1024,1024]{1,0:T(8,128)(2,1)} %param.23) | copy-start | bytes 6291460
  169.9 14.7 %copy-start.1 = (bf16[1024,1024]{1,0:T(8,128)(2,1)S(1)}, bf16[1024,1024]{1,0:T(8,128)(2,1)}, u32[]{:S(2)}) copy-start(bf16[1024,1024]{1,0:T(8,128)(2,1)} %param.21) | copy-start | bytes 6291460
Sparse Core Ops, SparseCore 0:
  60.1 47.0 all-gather.6
  108.7 45.8 all-gather.4
where the time goes:
time: 192 us; the launch traced here: 191 us
  waiting for transfers between devices  49.4 us (26%)
  blocking collectives  44.4 us (23%)
  matrix products  34.6 us (18%)
  local copies, waits for them, and re-layouts  33.1 us (17%)
  between operations  14.5 us (8%)
  starting transfers between devices  8.64 us (4%)
  other arithmetic  6.75 us (4%)
    all_gather x1, waiting for transfers between devices, per_device(): lax.all_gather(values, 'agent', axis=1, tiled=True)  29.7 us
    dot_general x1, matrix products, per_device(): jnp.dot(hidden, w_out, preferred_element_type=jnp.float32)  15 us
    all_to_all x1, blocking collectives, per_device(): lax.all_to_all(attended, 'tm', split_axis=0, concat_axis=2, tiled=True)  12.6 us
    all_to_all x1, blocking collectives, per_device(): lax.all_to_all(keys, 'tm', split_axis=2, concat_axis=0, tiled=True)  12.4 us
    ppermute x1, waiting for transfers between devices, shifted(): return lax.ppermute(shard, axis, pairs)  10.5 us
    unnamed x34, local copies, waits for them, and re-layouts  9.88 us
    unnamed x1, blocking collectives  9.79 us
    all_to_all x1, blocking collectives, per_device(): lax.all_to_all(values, 'tm', split_axis=2, concat_axis=0, tiled=True)  9.66 us
  transfers between devices with their start and end apart: 4, of which 4 were waited for; matrix products, arithmetic and copies ran while one was open for 15% of the time, Pallas kernels for 0%

commit v1 on v0

v1 whole, which is shorter than its diff:
```python
import functools

import jax
import jax.numpy as jnp
from jax import lax
from jax.experimental import pallas as pl
from jax.experimental.pallas import tpu as pltpu
from jax.sharding import PartitionSpec as P

HEAD = 64
EPS = 1e-05
LOG2E = 1.4426950408889634
MIB = 1024 * 1024
VMEM = pl.BlockSpec(memory_space=pltpu.VMEM)
ANY = pl.BlockSpec(memory_space=pl.ANY)
SMEM = pl.BlockSpec(memory_space=pltpu.SMEM)


def pinned(x):
    return pltpu.with_memory_space_constraint(x, pltpu.VMEM)


def dot(a, b):
    return jnp.dot(a, b, preferred_element_type=jnp.float32)


def dot_t(a, b):
    return lax.dot_general(a, b, (((1,), (1,)), ((), ())), preferred_element_type=jnp.float32)


def norm_scale(values):
    return lax.rsqrt(jnp.mean(values * values, axis=-1, keepdims=True) + EPS)


def gelu(x):
    return 0.5 * x * (1.0 + lax.erf(x * 0.7071067811865476))


def conv_kernel(steps, place, halo, tokens, taps, gain, *rest):
    outs, normed = rest[:steps], rest[steps]
    reach = taps.shape[0] - 1
    gains = gain[...]
    for step in range(steps):
        for part, base in ((halo, 0), (tokens, steps)):
            values = part[step].astype(jnp.float32)
            normed[base + step] = values * norm_scale(values) * gains
    z = place[0]
    for k in range(steps):
        step = z ^ k
        mixed = tokens[step].astype(jnp.float32)
        total = taps[0:1, :] * normed[steps + step]
        for lag in range(1, reach + 1):
            total = total + taps[lag : lag + 1, :] * normed[steps + step - lag]
        outs[k][...] = (mixed + total).astype(jnp.bfloat16)


def conv(place, halo, tokens, taps, gain):
    steps, agents, width = tokens.shape
    piece = jax.ShapeDtypeStruct((agents, width), jnp.bfloat16)
    return pl.pallas_call(
        functools.partial(conv_kernel, steps),
        out_shape=[piece] * steps,
        in_specs=[SMEM] + [VMEM] * 4,
        out_specs=[VMEM] * steps,
        scratch_shapes=[pltpu.VMEM((2 * steps, agents, width), jnp.float32)],
        compiler_params=pltpu.CompilerParams(vmem_limit_bytes=16 * MIB),
        cost_estimate=pl.CostEstimate(flops=10**7, bytes_accessed=2 * 10**6, transcendentals=0),
        name="conv",
    )(place, halo, tokens, taps, gain)


def feed_kernel(count, *refs):
    pieces = refs[:count]
    gain_in, gain_attn, w_in, w_out, w_query, w_key, w_value = refs[count : count + 7]
    query, keyval, second, hidden = refs[count + 7 :]
    first = jnp.concatenate([piece[...].astype(jnp.float32) for piece in pieces], axis=0)
    inner = (first * norm_scale(first) * gain_in[...]).astype(jnp.bfloat16)
    tile = 512
    for start in range(0, w_in.shape[1], tile):
        hidden[:, start : start + tile] = gelu(dot(inner, w_in[:, start : start + tile])).astype(jnp.bfloat16)
    total = (first + dot(hidden[...], w_out[...])).astype(jnp.bfloat16)
    second[...] = total
    values = total.astype(jnp.float32)
    attn_in = (values * norm_scale(values) * gain_attn[...]).astype(jnp.bfloat16)
    width = total.shape[1]
    query[...] = dot(attn_in, w_query[...]).astype(jnp.bfloat16)
    keyval[:, :width] = dot(attn_in, w_key[...]).astype(jnp.bfloat16)
    keyval[:, width:] = dot(attn_in, w_value[...]).astype(jnp.bfloat16)


def feed(pieces, gain_in, gain_attn, w_in, w_out, w_query, w_key, w_value):
    rows = sum(piece.shape[0] for piece in pieces)
    width = pieces[0].shape[1]
    return pl.pallas_call(
        functools.partial(feed_kernel, len(pieces)),
        out_shape=[
            jax.ShapeDtypeStruct((rows, width), jnp.bfloat16),
            jax.ShapeDtypeStruct((rows, 2 * width), jnp.bfloat16),
            jax.ShapeDtypeStruct((rows, width), jnp.bfloat16),
        ],
        in_specs=[VMEM] * (len(pieces) + 7),
        out_specs=[VMEM] * 3,
        scratch_shapes=[pltpu.VMEM((rows, w_in.shape[1]), jnp.bfloat16)],
        compiler_params=pltpu.CompilerParams(vmem_limit_bytes=16 * MIB),
        cost_estimate=pl.CostEstimate(flops=5 * 10**9, bytes_accessed=20 * 10**6, transcendentals=0),
        name="feed",
    )(*pieces, gain_in, gain_attn, pinned(w_in), pinned(w_out), pinned(w_query), pinned(w_key), pinned(w_value))


def attend_kernel(steps, others, place, info, query, second, w_output, *rest):
    blocks, outs = rest[: 1 + others], rest[1 + others : 1 + others + steps]
    bias, attended = rest[1 + others + steps :]
    rows, width = query.shape
    agents = rows // steps
    z, member, group, now = place[0], place[1], place[2], place[3]
    lane = lax.broadcasted_iota(jnp.int32, (agents, 128), 1)
    diagonal = lane == lax.broadcasted_iota(jnp.int32, (agents, 128), 0)
    first_half = lane < agents
    own_columns = []
    for k in range(steps):
        row = info[pl.ds(pl.multiple_of(8 * ((z ^ k) * group + member), 8), 8), :][0:1]
        own_columns.append(jnp.sum(jnp.where(diagonal, row, 0.0), axis=1, keepdims=True))
    own = jnp.concatenate(own_columns, axis=0)
    present_now = now.astype(jnp.float32)
    lane_row = lax.broadcasted_iota(jnp.int32, (1, 128), 1) < agents
    for r in range(1 + others):
        for pair in range(steps // 2):
            tiles = [
                info[pl.ds(pl.multiple_of(8 * ((z ^ k) * group + (member ^ r)), 8), 8), :]
                for k in (2 * pair, 2 * pair + 1)
            ]
            order = jnp.where(lane_row, tiles[0][0:1], tiles[1][0:1])
            present = jnp.where(lane_row, tiles[0][1:2], tiles[1][1:2])
            alive_order = jnp.where(present_now < present, order, 1e9)
            visible = (alive_order < own) | (order == own)
            start = r * rows + pair * 128
            bias[:, start : start + 128] = jnp.where(visible, 0.0, -1e30)
    scale = LOG2E * HEAD ** (-0.5)
    low = lax.broadcasted_iota(jnp.int32, (rows, 128), 1) < HEAD
    ones = jnp.ones((rows, 128), jnp.bfloat16)
    for head_pair in range(width // 128):
        columns = slice(128 * head_pair, 128 * head_pair + 128)
        value_columns = slice(width + 128 * head_pair, width + 128 * head_pair + 128)
        queries = query[:, columns]
        results = []
        for half in (low, ~low):
            masked = jnp.where(half, queries, jnp.zeros_like(queries))
            scores = [
                dot_t(masked, block[:, columns]) * scale + bias[:, r * rows : (r + 1) * rows]
                for r, block in enumerate(blocks)
            ]
            top = functools.reduce(jnp.maximum, [jnp.max(s, axis=1, keepdims=True) for s in scores])
            total = None
            for s, block in zip(scores, blocks):
                weights = jnp.exp2(s - top).astype(jnp.bfloat16)
                part = dot(weights, jnp.concatenate([block[:, value_columns], ones], axis=1))
                total = part if total is None else total + part
            results.append(total[:, :128] / total[:, 128:])
        attended[:, columns] = jnp.where(low, results[0], results[1]).astype(jnp.bfloat16)
    result = second[...].astype(jnp.float32) + dot(attended[...], w_output[...])
    for k in range(steps):
        outs[k][...] = result[k * agents : (k + 1) * agents].astype(jnp.bfloat16)


def attend(place, info, query, second, w_output, blocks, steps):
    rows, width = query.shape
    piece = jax.ShapeDtypeStruct((rows // steps, width), jnp.bfloat16)
    return pl.pallas_call(
        functools.partial(attend_kernel, steps, len(blocks) - 1),
        out_shape=[piece] * steps,
        in_specs=[SMEM] + [VMEM] * (4 + len(blocks)),
        out_specs=[VMEM] * steps,
        scratch_shapes=[
            pltpu.VMEM((rows, rows * len(blocks)), jnp.float32),
            pltpu.VMEM((rows, width), jnp.bfloat16),
        ],
        compiler_params=pltpu.CompilerParams(vmem_limit_bytes=24 * MIB),
        cost_estimate=pl.CostEstimate(flops=4 * 10**9, bytes_accessed=6 * 10**6, transcendentals=2 * 10**6),
        name="attend",
    )(place, info, query, second, pinned(w_output), *blocks)


def place_kernel(steps, place, *refs):
    pieces, out = refs[:steps], refs[steps]
    for k in range(steps):
        out[place[0] ^ k] = pieces[k][...]


def put_back(place, pieces):
    steps = len(pieces)
    agents, width = pieces[0].shape
    return pl.pallas_call(
        functools.partial(place_kernel, steps),
        out_shape=jax.ShapeDtypeStruct((steps, agents, width), jnp.bfloat16),
        in_specs=[SMEM] + [VMEM] * steps,
        out_specs=VMEM,
        compiler_params=pltpu.CompilerParams(vmem_limit_bytes=8 * MIB),
        name="put_back",
    )(place, *pieces)


def per_device(
    tokens,
    conv_taps,
    norm_first,
    norm_second,
    norm_third,
    w_in,
    w_out,
    w_query,
    w_key,
    w_value,
    w_output,
    agent_order,
    present_steps,
):
    steps, agents, width = tokens.shape
    tm_count, count = lax.axis_size("tm"), lax.axis_size("agent")
    group = count // steps
    assert group * steps == count and steps == 4 and agents == 64
    spot = lax.axis_index("agent")
    z, member = spot // group, spot % group
    now = lax.axis_index("tm") * steps + z
    place = jnp.stack([z, member, jnp.int32(group), now]).astype(jnp.int32)

    def across(x, k):
        return lax.ppermute(x, "agent", [(i, ((i // group) ^ k) * group + i % group) for i in range(count)])

    def within(x, r):
        return lax.ppermute(x, "agent", [(i, (i // group) * group + ((i % group) ^ r)) for i in range(count)])

    halo = lax.ppermute(tokens, "tm", [(i, i + 1) for i in range(tm_count - 1)])
    rows = jnp.stack([agent_order, present_steps]).astype(jnp.float32)
    info = jnp.pad(jnp.concatenate([rows, rows], axis=1), ((0, 6), (0, 0)))
    info = lax.all_gather(info, "agent", axis=0, tiled=True)
    pieces = conv(place, halo, tokens, conv_taps, norm_first.reshape(1, width))
    pieces = [pieces[0]] + [across(pieces[k], k) for k in range(1, steps)]
    query, keyval, second = feed(
        pieces, norm_second.reshape(1, width), norm_third.reshape(1, width), w_in, w_out, w_query, w_key, w_value
    )
    blocks = [keyval] + [within(keyval, r) for r in range(1, group)]
    results = attend(place, info, query, second, w_output, blocks, steps)
    results = [results[0]] + [across(results[k], k) for k in range(1, steps)]
    return put_back(place, results)


def solution(mesh):
    in_specs = (P("tm", "agent", None),) + (P(),) * 10 + (P("agent"), P("agent"))
    return jax.shard_map(
        per_device, mesh=mesh, in_specs=in_specs, out_specs=P("tm", "agent", None), check_vma=False
    )
```

time: 192 us -> 87.3 us (0.45)
  the two profiles are of different devices: /device:TPU:0 before, /device:TPU:12 now
where the time goes in v1:
time: 87.3 us; the launch traced here: 86.7 us
  waiting for transfers between devices  35.8 us (41%)
  local copies, waits for them, and re-layouts  14.2 us (16%)
  Pallas kernels  13.1 us (15%)
  blocking collectives  12.7 us (15%)
  starting transfers between devices  10.6 us (12%)
    ppermute x6, waiting for transfers between devices, across(): lax.ppermute(x, 'agent', [(i, (i // group ^ k) * group + i % group) for i...  22.7 us
    unnamed x26, local copies, waits for them, and re-layouts  14.2 us
    ppermute x1, waiting for transfers between devices, per_device(): halo = lax.ppermute(tokens, 'tm', [(i, i + 1) for i in range(tm_count - 1)])  13.2 us
    all_gather x1, blocking collectives, per_device(): info = lax.all_gather(info, 'agent', axis=0, tiled=True)  12.7 us
    ppermute x6, starting transfers between devices, across(): lax.ppermute(x, 'agent', [(i, (i // group ^ k) * group + i % group) for i...  7.14 us
    pallas_call x1, Pallas kernels, feed(): pl.pallas_call(functools.partial(feed_kernel, len(pieces)), out_shape=[ja...  5.58 us
    pallas_call x1, Pallas kernels, attend(): pl.pallas_call(functools.partial(attend_kernel, steps, len(blocks) - 1),...  4.53 us
    ppermute x1, starting transfers between devices, per_device(): halo = lax.ppermute(tokens, 'tm', [(i, i + 1) for i in range(tm_count - 1)])  3.39 us
  transfers between devices with their start and end apart: 8, of which 7 were waited for; matrix products, arithmetic and copies ran while one was open for 0% of the time, Pallas kernels for 0%

profile of v1, /device:TPU:12, one launch (start us, length us, event | category | flops | bytes accessed | tf_op | source)
XLA Modules:
  0.0 86.7 jit_solution(15336682772784045118)
XLA Ops:
  0.0 3.4 %collective-permute-start = (bf16[4,64,1024]{2,1,0:T(8,128)(2,1)}, bf16[4,64,1024]{2,1,0:T(8,128)(2,1)S(1)}, u32[]{:S(2)}, u32[]{:S(2)}) collective-permute-start(bf16[4,64,1024]{2,1,0:T(8,128)(2,1)} %tokens.1), channel_id=1, source_target_pairs={{0,8},{8,16},{16,24},{1,9},{9,17},{17,25},{2,10},{10,18},{18,26},{... | collective-permute-start | bytes 1572872 | tf_op jit(solution)/shard_map/ppermute | solution.py:232
  3.4 0.1 pad_add_fusion.place
  3.5 13.2 %collective-permute-done.halo = bf16[4,64,1024]{2,1,0:T(8,128)(2,1)S(1)} collective-permute-done((bf16[4,64,1024]{2,1,0:T(8,128)(2,1)}, bf16[4,64,1024]{2,1,0:T(8,128)(2,1)S(1)}, u32[]{:S(2)}, u32[]{:S(2)}) %collective-permute-start) | collective-permute-done | bytes 524320 | tf_op jit(solution)/shard_map/ppermute | solution.py:232
  16.7 0.0 copy-start.5
  16.7 1.0 %copy-done.5 = bf16[4,64,1024]{2,1,0:T(8,128)(2,1)S(1)} copy-done((bf16[4,64,1024]{2,1,0:T(8,128)(2,1)S(1)}, bf16[4,64,1024]{2,1,0:T(8,128)(2,1)}, u32[]{:S(2)}) %copy-start.5) | copy-done | bytes 524312
  17.7 0.0 copy-start.6
  17.7 0.8 copy-done.6
  18.5 0.0 copy-start.7
  18.5 0.7 copy-done.7
  19.1 1.7 %conv.1 = (bf16[64,1024]{1,0:T(8,128)(2,1)S(1)}, bf16[64,1024]{1,0:T(8,128)(2,1)S(1)}, bf16[64,1024]{1,0:T(8,128)(2,1)S(1)}, bf16[64,1024]{1,0:T(8,128)(2,1)S(1)}) custom-call(s32[4]{0:T(128)S(1)} %pad_add_fusion.place, bf16[4,64,1024]{2,1,0:T(8,128)(2,1)S(1)} %collective-permute-done.halo, bf16[4,64,1024]{2,1,0:T(8,128)(2,1)S(1)} %copy-done.5, ...), custom_call_target="tpu_custom_call" | custom-call | flops 10000000 | bytes 2000000 | tf_op jit(solution)/shard_map/conv/pallas_call | solution.py:60
  20.8 0.5 collective-permute-start.1
  21.3 2.6 %collective-permute-start.2 = (bf16[64,1024]{1,0:T(8,128)(2,1)S(1)}, bf16[64,1024]{1,0:T(8,128)(2,1)S(1)}, u32[]{:S(2)}, u32[]{:S(2)}) collective-permute-start(bf16[64,1024]{1,0:T(8,128)(2,1)S(1)} %get-tuple-element.18), channel_id=1, source_target_pairs={{0,4},{1,5},{2,6},{3,7},{4,0},{5,1},{6,2},{7,3},{8,12},{9,13},{10,... | collective-permute-start | bytes 393224 | tf_op jit(solution)/shard_map/ppermute | solution.py:227
  23.9 0.5 collective-permute-start.3
  24.4 2.6 %collective-permute-done.1.refs_1_ = bf16[64,1024]{1,0:T(8,128)(2,1)S(1)} collective-permute-done((bf16[64,1024]{1,0:T(8,128)(2,1)S(1)}, bf16[64,1024]{1,0:T(8,128)(2,1)S(1)}, u32[]{:S(2)}, u32[]{:S(2)}) %collective-permute-start.1) | collective-permute-done | bytes 131104 | tf_op jit(solution)/shard_map/ppermute | solution.py:227
  26.9 5.6 %collective-permute-done.2.refs_2_ = bf16[64,1024]{1,0:T(8,128)(2,1)S(1)} collective-permute-done((bf16[64,1024]{1,0:T(8,128)(2,1)S(1)}, bf16[64,1024]{1,0:T(8,128)(2,1)S(1)}, u32[]{:S(2)}, u32[]{:S(2)}) %collective-permute-start.2) | collective-permute-done | bytes 131104 | tf_op jit(solution)/shard_map/ppermute | solution.py:227
  32.6 2.3 %collective-permute-done.3.refs_3_ = bf16[64,1024]{1,0:T(8,128)(2,1)S(1)} collective-permute-done((bf16[64,1024]{1,0:T(8,128)(2,1)S(1)}, bf16[64,1024]{1,0:T(8,128)(2,1)S(1)}, u32[]{:S(2)}, u32[]{:S(2)}) %collective-permute-start.3) | collective-permute-done | bytes 131104 | tf_op jit(solution)/shard_map/ppermute | solution.py:227
  34.9 0.0 copy-start
  34.9 2.8 %copy-done = bf16[1024,3072]{1,0:T(8,128)(2,1)S(1)} copy-done((bf16[1024,3072]{1,0:T(8,128)(2,1)S(1)}, bf16[1024,3072]{1,0:T(8,128)(2,1)}, u32[]{:S(2)}) %copy-start) | copy-done | bytes 6291480
  37.7 0.0 copy-start.1
  37.7 2.8 %copy-done.1 = bf16[3072,1024]{1,0:T(8,128)(2,1)S(1)} copy-done((bf16[3072,1024]{1,0:T(8,128)(2,1)S(1)}, bf16[3072,1024]{1,0:T(8,128)(2,1)}, u32[]{:S(2)}) %copy-start.1) | copy-done | bytes 6291480
  40.5 0.0 copy-start.2
  40.5 1.6 %copy-done.2 = bf16[1024,1024]{1,0:T(8,128)(2,1)S(1)} copy-done((bf16[1024,1024]{1,0:T(8,128)(2,1)S(1)}, bf16[1024,1024]{1,0:T(8,128)(2,1)}, u32[]{:S(2)}) %copy-start.2) | copy-done | bytes 2097176
  42.1 0.0 copy-start.3
  42.1 1.6 %copy-done.3 = bf16[1024,1024]{1,0:T(8,128)(2,1)S(1)} copy-done((bf16[1024,1024]{1,0:T(8,128)(2,1)S(1)}, bf16[1024,1024]{1,0:T(8,128)(2,1)}, u32[]{:S(2)}) %copy-start.3) | copy-done | bytes 2097176
  43.6 0.0 copy-start.4
  43.6 1.6 %copy-done.4 = bf16[1024,1024]{1,0:T(8,128)(2,1)S(1)} copy-done((bf16[1024,1024]{1,0:T(8,128)(2,1)S(1)}, bf16[1024,1024]{1,0:T(8,128)(2,1)}, u32[]{:S(2)}) %copy-start.4) | copy-done | bytes 2097176
  45.2 0.0 copy-start.8
  45.2 0.7 copy-done.8
  45.9 0.0 copy-start.9
  45.9 0.7 copy-done.9
  46.6 0.0 copy-start.12
  46.6 0.0 copy-start.10
  46.6 5.6 %feed.1 = (bf16[256,1024]{1,0:T(8,128)(2,1)S(1)}, bf16[256,2048]{1,0:T(8,128)(2,1)S(1)}, bf16[256,1024]{1,0:T(8,128)(2,1)S(1)}) custom-call(bf16[64,1024]{1,0:T(8,128)(2,1)S(1)} %get-tuple-element.16.refs_0_, bf16[64,1024]{1,0:T(8,128)(2,1)S(1)} %collective-permute-done.1.refs_1_, bf16[64,1024]{1,0:T(8,128)(2,1)S(1)} %collective-permute-done.2.refs_2_, ...), custom_call_target="tpu_custom_call" | custom-call | flops 5000000000 | bytes 20000000 | tf_op jit(solution)/shard_map/feed/pallas_call | solution.py:94
  52.2 0.1 collective-permute-start.4
  52.3 0.0 copy-done.11
  52.3 0.0 copy-done.12
  52.3 0.1 select_maximum_fusion
  52.4 12.7 %all_gather.3.info = f32[64,128]{1,0:T(8,128)S(1)} all-gather(f32[8,128]{1,0:T(8,128)S(1)} %select_maximum_fusion), channel_id=1, replica_groups=mesh['tm'=4,'agent'=8] {'agent'}, dimensions={0}, use_global_device_ids=true | all-gather | bytes 36864 | tf_op jit(solution)/shard_map/all_gather | solution.py:235
  65.1 0.0 collective-permute-done.4.rest_1_
  65.1 0.0 copy-done.10
  65.1 4.5 %attend.1 = (bf16[64,1024]{1,0:T(8,128)(2,1)S(1)}, bf16[64,1024]{1,0:T(8,128)(2,1)S(1)}, bf16[64,1024]{1,0:T(8,128)(2,1)S(1)}, bf16[64,1024]{1,0:T(8,128)(2,1)S(1)}) custom-call(s32[4]{0:T(128)S(1)} %pad_add_fusion.place, f32[64,128]{1,0:T(8,128)S(1)} %all_gather.3.info, bf16[256,1024]{1,0:T(8,128)(2,1)S(1)} %get-tuple-element.20.query, ...), custom_call_target="tpu_custom_call" | custom-call | flops 4000000000 | bytes 6000000 | tf_op jit(solution)/shard_map/attend/pallas_call | solution.py:168
  69.6 2.0 %collective-permute-start.5 = (bf16[64,1024]{1,0:T(8,128)(2,1)S(1)}, bf16[64,1024]{1,0:T(8,128)(2,1)S(1)}, u32[]{:S(2)}, u32[]{:S(2)}) collective-permute-start(bf16[64,1024]{1,0:T(8,128)(2,1)S(1)} %get-tuple-element.24), channel_id=1, source_target_pairs={{0,2},{1,3},{2,0},{3,1},{4,6},{5,7},{6,4},{7,5},{8,10},{9,11},{10,... | collective-permute-start | bytes 393224 | tf_op jit(solution)/shard_map/ppermute | solution.py:227
  71.7 0.6 collective-permute-start.6
  72.2 1.0 %collective-permute-start.7 = (bf16[64,1024]{1,0:T(8,128)(2,1)S(1)}, bf16[64,1024]{1,0:T(8,128)(2,1)S(1)}, u32[]{:S(2)}, u32[]{:S(2)}) collective-permute-start(bf16[64,1024]{1,0:T(8,128)(2,1)S(1)} %get-tuple-element.26), channel_id=1, source_target_pairs={{0,6},{1,7},{2,4},{3,5},{4,2},{5,3},{6,0},{7,1},{8,14},{9,15},{10,... | collective-permute-start | bytes 393224 | tf_op jit(solution)/shard_map/ppermute | solution.py:227
  73.2 3.7 %collective-permute-done.5.refs_1_ = bf16[64,1024]{1,0:T(8,128)(2,1)S(1)} collective-permute-done((bf16[64,1024]{1,0:T(8,128)(2,1)S(1)}, bf16[64,1024]{1,0:T(8,128)(2,1)S(1)}, u32[]{:S(2)}, u32[]{:S(2)}) %collective-permute-start.5) | collective-permute-done | bytes 131104 | tf_op jit(solution)/shard_map/ppermute | solution.py:227
  76.9 4.9 %collective-permute-done.6.refs_2_ = bf16[64,1024]{1,0:T(8,128)(2,1)S(1)} collective-permute-done((bf16[64,1024]{1,0:T(8,128)(2,1)S(1)}, bf16[64,1024]{1,0:T(8,128)(2,1)S(1)}, u32[]{:S(2)}, u32[]{:S(2)}) %collective-permute-start.6) | collective-permute-done | bytes 131104 | tf_op jit(solution)/shard_map/ppermute | solution.py:227
  81.8 3.6 %collective-permute-done.7.refs_3_ = bf16[64,1024]{1,0:T(8,128)(2,1)S(1)} collective-permute-done((bf16[64,1024]{1,0:T(8,128)(2,1)S(1)}, bf16[64,1024]{1,0:T(8,128)(2,1)S(1)}, u32[]{:S(2)}, u32[]{:S(2)}) %collective-permute-start.7) | collective-permute-done | bytes 131104 | tf_op jit(solution)/shard_map/ppermute | solution.py:227
  85.4 1.4 %put_back.1 = bf16[4,64,1024]{2,1,0:T(8,128)(2,1)} custom-call(s32[4]{0:T(128)S(1)} %pad_add_fusion.place, bf16[64,1024]{1,0:T(8,128)(2,1)S(1)} %get-tuple-element.23.refs_0_, bf16[64,1024]{1,0:T(8,128)(2,1)S(1)} %collective-permute-done.5.refs_1_, bf16[64,1024]{1,0:T(8,128)(2,1)S(1)} %collective-permute-done.6.refs_2_, ...), custom_call_target="tpu_custom_call" | custom-call | tf_op jit(solution)/shard_map/put_back/pallas_call | solution.py:192
  (2 shorter events, 0.0 us)
Async XLA Ops:
  0.0 16.7 %collective-permute-start = (bf16[4,64,1024]{2,1,0:T(8,128)(2,1)}, bf16[4,64,1024]{2,1,0:T(8,128)(2,1)S(1)}, u32[]{:S(2)}, u32[]{:S(2)}) collective-permute-start(bf16[4,64,1024]{2,1,0:T(8,128)(2,1)} %tokens.1), channel_id=1, source_target_pairs={{0,8},{8,16},{16,24},{1,9},{9,17},{17,25},{2,10},{10,18},{18,26},{... | collective-permute-start | bytes 1572872 | tf_op jit(solution)/shard_map/ppermute | solution.py:232
  16.7 1.0 %copy-start.5 = (bf16[4,64,1024]{2,1,0:T(8,128)(2,1)S(1)}, bf16[4,64,1024]{2,1,0:T(8,128)(2,1)}, u32[]{:S(2)}) copy-start(bf16[4,64,1024]{2,1,0:T(8,128)(2,1)} %tokens.1) | copy-start | bytes 1572868
  17.7 0.8 copy-start.6
  18.5 0.7 copy-start.7
  20.8 6.1 %collective-permute-start.1 = (bf16[64,1024]{1,0:T(8,128)(2,1)S(1)}, bf16[64,1024]{1,0:T(8,128)(2,1)S(1)}, u32[]{:S(2)}, u32[]{:S(2)}) collective-permute-start(bf16[64,1024]{1,0:T(8,128)(2,1)S(1)} %get-tuple-element.17), channel_id=1, source_target_pairs={{0,2},{1,3},{2,0},{3,1},{4,6},{5,7},{6,4},{7,5},{8,10},{9,11},{10,... | collective-permute-start | bytes 393224 | tf_op jit(solution)/shard_map/ppermute | solution.py:227
  21.3 11.3 %collective-permute-start.2 = (bf16[64,1024]{1,0:T(8,128)(2,1)S(1)}, bf16[64,1024]{1,0:T(8,128)(2,1)S(1)}, u32[]{:S(2)}, u32[]{:S(2)}) collective-permute-start(bf16[64,1024]{1,0:T(8,128)(2,1)S(1)} %get-tuple-element.18), channel_id=1, source_target_pairs={{0,4},{1,5},{2,6},{3,7},{4,0},{5,1},{6,2},{7,3},{8,12},{9,13},{10,... | collective-permute-start | bytes 393224 | tf_op jit(solution)/shard_map/ppermute | solution.py:227
  23.9 11.0 %collective-permute-start.3 = (bf16[64,1024]{1,0:T(8,128)(2,1)S(1)}, bf16[64,1024]{1,0:T(8,128)(2,1)S(1)}, u32[]{:S(2)}, u32[]{:S(2)}) collective-permute-start(bf16[64,1024]{1,0:T(8,128)(2,1)S(1)} %get-tuple-element.19), channel_id=1, source_target_pairs={{0,6},{1,7},{2,4},{3,5},{4,2},{5,3},{6,0},{7,1},{8,14},{9,15},{10,... | collective-permute-start | bytes 393224 | tf_op jit(solution)/shard_map/ppermute | solution.py:227
  34.9 2.8 %copy-start = (bf16[1024,3072]{1,0:T(8,128)(2,1)S(1)}, bf16[1024,3072]{1,0:T(8,128)(2,1)}, u32[]{:S(2)}) copy-start(bf16[1024,3072]{1,0:T(8,128)(2,1)} %refs_6_.1) | copy-start | bytes 18874372
  37.7 2.8 %copy-start.1 = (bf16[3072,1024]{1,0:T(8,128)(2,1)S(1)}, bf16[3072,1024]{1,0:T(8,128)(2,1)}, u32[]{:S(2)}) copy-start(bf16[3072,1024]{1,0:T(8,128)(2,1)} %refs_7_.1) | copy-start | bytes 18874372
  40.5 1.6 %copy-start.2 = (bf16[1024,1024]{1,0:T(8,128)(2,1)S(1)}, bf16[1024,1024]{1,0:T(8,128)(2,1)}, u32[]{:S(2)}) copy-start(bf16[1024,1024]{1,0:T(8,128)(2,1)} %refs_8_.1) | copy-start | bytes 6291460
  42.1 1.6 %copy-start.3 = (bf16[1024,1024]{1,0:T(8,128)(2,1)S(1)}, bf16[1024,1024]{1,0:T(8,128)(2,1)}, u32[]{:S(2)}) copy-start(bf16[1024,1024]{1,0:T(8,128)(2,1)} %refs_9_.1) | copy-start | bytes 6291460
  43.6 1.6 %copy-start.4 = (bf16[1024,1024]{1,0:T(8,128)(2,1)S(1)}, bf16[1024,1024]{1,0:T(8,128)(2,1)}, u32[]{:S(2)}) copy-start(bf16[1024,1024]{1,0:T(8,128)(2,1)} %refs_10_.1) | copy-start | bytes 6291460
  45.2 0.7 copy-start.8
  45.9 0.7 copy-start.9
  46.6 5.7 %copy-start.11 = (s32[64]{0:T(128)S(1)}, s32[64]{0:T(128)}, u32[]{:S(2)}) copy-start(s32[64]{0:T(128)} %param.25) | copy-start | bytes 772
  46.6 5.7 %copy-start.12 = (s32[64]{0:T(128)S(1)}, s32[64]{0:T(128)}, u32[]{:S(2)}) copy-start(s32[64]{0:T(128)} %param.24) | copy-start | bytes 772
  46.6 18.5 %copy-start.10 = (bf16[1024,1024]{1,0:T(8,128)(2,1)S(1)}, bf16[1024,1024]{1,0:T(8,128)(2,1)}, u32[]{:S(2)}) copy-start(bf16[1024,1024]{1,0:T(8,128)(2,1)} %w_output.1) | copy-start | bytes 6291460
  52.2 12.9 %collective-permute-start.4 = (bf16[256,2048]{1,0:T(8,128)(2,1)S(1)}, bf16[256,2048]{1,0:T(8,128)(2,1)S(1)}, u32[]{:S(2)}, u32[]{:S(2)}) collective-permute-start(bf16[256,2048]{1,0:T(8,128)(2,1)S(1)} %get-tuple-element.22.rest_0_), channel_id=1, source_target_pairs={{0,1},{1,0},{2,3},{3,2},{4,5},{5,4},{6,7},{7,6},{8,9},{9,8},{10,11... | collective-permute-start | bytes 3145736 | tf_op jit(solution)/shard_map/ppermute | solution.py:230
  69.6 7.3 %collective-permute-start.5 = (bf16[64,1024]{1,0:T(8,128)(2,1)S(1)}, bf16[64,1024]{1,0:T(8,128)(2,1)S(1)}, u32[]{:S(2)}, u32[]{:S(2)}) collective-permute-start(bf16[64,1024]{1,0:T(8,128)(2,1)S(1)} %get-tuple-element.24), channel_id=1, source_target_pairs={{0,2},{1,3},{2,0},{3,1},{4,6},{5,7},{6,4},{7,5},{8,10},{9,11},{10,... | collective-permute-start | bytes 393224 | tf_op jit(solution)/shard_map/ppermute | solution.py:227
  71.7 10.1 %collective-permute-start.6 = (bf16[64,1024]{1,0:T(8,128)(2,1)S(1)}, bf16[64,1024]{1,0:T(8,128)(2,1)S(1)}, u32[]{:S(2)}, u32[]{:S(2)}) collective-permute-start(bf16[64,1024]{1,0:T(8,128)(2,1)S(1)} %get-tuple-element.25), channel_id=1, source_target_pairs={{0,4},{1,5},{2,6},{3,7},{4,0},{5,1},{6,2},{7,3},{8,12},{9,13},{10,... | collective-permute-start | bytes 393224 | tf_op jit(solution)/shard_map/ppermute | solution.py:227
  72.2 13.1 %collective-permute-start.7 = (bf16[64,1024]{1,0:T(8,128)(2,1)S(1)}, bf16[64,1024]{1,0:T(8,128)(2,1)S(1)}, u32[]{:S(2)}, u32[]{:S(2)}) collective-permute-start(bf16[64,1024]{1,0:T(8,128)(2,1)S(1)} %get-tuple-element.26), channel_id=1, source_target_pairs={{0,6},{1,7},{2,4},{3,5},{4,2},{5,3},{6,0},{7,1},{8,14},{9,15},{10,... | collective-permute-start | bytes 393224 | tf_op jit(solution)/shard_map/ppermute | solution.py:227
